TPU v7x, 512 devices: a whole 4x8x8 slice. The times are simulated.
512 devices in a mesh: ctx: 64 (over y_lo, z, x), tp: 8 (over y_hi, core).
Axes of the slice: x: 4, y: 8 (y_hi: 4, y_lo: 2; y = y_hi * 2 + y_lo), z: 8, core: 2. Of those that a mesh axis runs over, the one named last changes fastest.
Arguments:
- queries: bfloat16 [16384, 8192], P('ctx', 'tp'), may hold values from -128 to 128
- cotangent: bfloat16 [16384, 8192], P('ctx', 'tp'), may hold values from -96 to 96
- image_keys: bfloat16 [64, 64, 1024], P('ctx', None, 'tp'), may hold values from -8 to 8
- image_values: bfloat16 [64, 64, 1024], P('ctx', None, 'tp'), may hold values from -6 to 6
- attn_gate: float32 [1], replicated, may hold values from 0.4 to 1.5
- block_mask: int32 [128, 64], P('ctx'), may hold values from 0 to 1, as said below
- image_owner: int32 [64], replicated, may hold values from 0 to 63, each once
Outputs:
- query_grad: bfloat16 [16384, 8192], P('ctx', 'tp')
- key_grad: bfloat16 [64, 64, 1024], P('ctx', None, 'tp')
- value_grad: bfloat16 [64, 64, 1024], P('ctx', None, 'tp')
- gate_grad: float32 [1], replicated
Inputs may be any that keep to these rules, and one draw needn't show every extreme that they name: `block_mask`: every text block reads at least one image; the 2 blocks of one index of ctx together read exactly 32 distinct images.
All inputs are finite; a program needn't handle non-finite values.
Results may differ from a plain program's by a relative error of at most 0.02.
Values may be sent and summed in bfloat16 or wider, within the bound.
A program may use at most 64 MiB of HBM per device.

v0:
```python
import math
import jax
import jax.numpy as jnp
from jax import lax
from jax.sharding import PartitionSpec as P

HD = 128
BLK = 128


def per_device(queries, cotangent, image_keys, image_values, attn_gate, block_mask, image_owner):
    tok_dev = queries.shape[0]
    local_kv = image_keys.shape[2] // HD
    local_heads = queries.shape[1] // HD
    groups = local_heads // local_kv
    img_tok = image_keys.shape[1]
    inv_root = 1.0 / math.sqrt(HD)
    read_most = lax.axis_size("ctx") // 2
    gathered_keys, gathered_values = (
        lax.all_gather(image_keys, "ctx", axis=0, tiled=True),
        lax.all_gather(image_values, "ctx", axis=0, tiled=True),
    )
    n_images = gathered_keys.shape[0]
    read_any = jnp.max(block_mask, axis=0)
    ranking = read_any * (2 * n_images) + (n_images - 1 - jnp.arange(n_images, dtype=jnp.int32))
    top_vals, image_ids = lax.top_k(ranking, read_most)
    is_read = read_any[image_ids] > 0
    slot_ids = image_owner[image_ids]
    block_keep = (block_mask[:, image_ids] > 0) & is_read[None, :]
    keep_mask = jnp.repeat(jnp.repeat(block_keep, BLK, axis=0), img_tok, axis=1)
    key_rows = jnp.take(gathered_keys, slot_ids, axis=0).reshape(read_most * img_tok, local_kv, HD)
    value_rows = jnp.take(gathered_values, slot_ids, axis=0).reshape(
        read_most * img_tok, local_kv, HD
    )
    query_heads = queries.reshape(tok_dev, local_kv, groups, HD).transpose(2, 0, 1, 3)
    cot_heads = cotangent.reshape(tok_dev, local_kv, groups, HD).transpose(2, 0, 1, 3)
    gate_value = jnp.tanh(attn_gate[0])

    def head_step(state_in, head_inputs):
        key_acc, value_acc, gate_acc = state_in
        query_one, cot_one = head_inputs
        scores = (
            jnp.einsum("tkd,skd->kts", query_one, key_rows, preferred_element_type=jnp.float32)
            * inv_root
        )
        scores = jnp.where(keep_mask, scores, -1e30)
        row_max = jnp.max(scores, axis=-1, keepdims=True)
        exp_terms = jnp.where(keep_mask, jnp.exp(scores - row_max), 0.0)
        prob_full = exp_terms / jnp.sum(exp_terms, axis=-1, keepdims=True)
        prob_half = prob_full.astype(jnp.bfloat16)
        attended = jnp.einsum(
            "kts,skd->tkd", prob_half, value_rows, preferred_element_type=jnp.float32
        )
        cot_f = cot_one.astype(jnp.float32)
        gate_part = jnp.sum(cot_f * attended)
        attn_grad = (gate_value * cot_f).astype(jnp.bfloat16)
        prob_grad = jnp.einsum(
            "tkd,skd->kts", attn_grad, value_rows, preferred_element_type=jnp.float32
        )
        row_delta = jnp.sum(attn_grad.astype(jnp.float32) * attended, axis=-1).T
        score_grad = (prob_full * (prob_grad - row_delta[:, :, None]) * inv_root).astype(
            jnp.bfloat16
        )
        query_grad = jnp.einsum(
            "kts,skd->tkd", score_grad, key_rows, preferred_element_type=jnp.float32
        ).astype(jnp.bfloat16)
        key_acc = key_acc + jnp.einsum(
            "kts,tkd->skd", score_grad, query_one, preferred_element_type=jnp.float32
        )
        value_acc = value_acc + jnp.einsum(
            "kts,tkd->skd", prob_half, attn_grad, preferred_element_type=jnp.float32
        )
        return ((key_acc, value_acc, gate_acc + gate_part), query_grad)

    zero_grads = jnp.zeros((read_most * img_tok, local_kv, HD), jnp.float32)
    init_state = (zero_grads, zero_grads, jnp.zeros((), jnp.float32))
    (key_acc, value_acc, gate_acc), head_grads = lax.scan(
        head_step, init_state, (query_heads, cot_heads)
    )
    query_grad = head_grads.transpose(1, 2, 0, 3).reshape(tok_dev, local_heads * HD)
    stacked = jnp.concatenate(
        [
            key_acc.reshape(read_most, img_tok, local_kv * HD),
            value_acc.reshape(read_most, img_tok, local_kv * HD),
        ],
        axis=-1,
    )
    stacked = jnp.where(is_read[:, None, None], stacked, 0.0)
    buffer = (
        jnp.zeros((n_images, img_tok, 2 * local_kv * HD), jnp.float32).at[slot_ids].add(stacked)
    )
    received = lax.all_to_all(buffer, "ctx", split_axis=0, concat_axis=0, tiled=True)
    summed = jnp.sum(received, axis=0, keepdims=True)
    key_grad = summed[:, :, : local_kv * HD].astype(jnp.bfloat16)
    value_grad = summed[:, :, local_kv * HD :].astype(jnp.bfloat16)
    gate_total = lax.psum(gate_acc, ("ctx", "tp"))
    term_count = tok_dev * lax.axis_size("ctx") * local_heads * lax.axis_size("tp") * HD
    gate_grad = ((1.0 - gate_value * gate_value) * gate_total / math.sqrt(term_count)).reshape(1)
    return (query_grad, key_grad, value_grad, gate_grad)


def solution(mesh):
    in_specs = (
        P("ctx", "tp"),
        P("ctx", "tp"),
        P("ctx", None, "tp"),
        P("ctx", None, "tp"),
        P(),
        P("ctx", None),
        P(),
    )
    out_specs = (P("ctx", "tp"), P("ctx", None, "tp"), P("ctx", None, "tp"), P())
    return jax.shard_map(
        per_device, mesh=mesh, in_specs=in_specs, out_specs=out_specs, check_vma=False
    )
```

profile of v0, /device:TPU:1, one launch (start us, length us, event | category | flops | bytes accessed | tf_op | source)
XLA Modules:
  0.0 885.6 jit_solution(12151461978923027463)
XLA Ops:
  10.9 2.0 top_k.11
  17.4 253.3 %all-gather.5.cloned.1.call-done = bf16[64,64,128]{2,1,0:T(8,128)(2,1)} async-done(((bf16[1,64,128]{2,1,0:T(8,128)(2,1)}), bf16[64,64,128]{2,1,0:T(8,128)(2,1)}) %all-gather.5.cloned.1.call-update) | async-done | bytes 1048592 | tf_op jit(solution)/shard_map/all_gather | solution.py:21
  270.7 1.9 gather_fusion.4
  272.6 297.7 %all-gather.3.cloned.1.call-done = bf16[64,64,128]{2,1,0:T(8,128)(2,1)} async-done(((bf16[1,64,128]{2,1,0:T(8,128)(2,1)}), bf16[64,64,128]{2,1,0:T(8,128)(2,1)}) %all-gather.3.cloned.1.call-update) | async-done | bytes 1048592 | tf_op jit(solution)/shard_map/all_gather | solution.py:20
  570.4 1.9 gather_fusion.3
  572.4 92.9 %while.17 = (s32[]{:T(128)}, f32[2048,1,128]{0,2,1:T(8,128)}, f32[2048,1,128]{0,2,1:T(8,128)}, f32[]{:T(128)}, bf16[8,256,1,128]{3,1,2,0:T(8,128)(2,1)}, /*index...) while((s32[]{:T(128)}, f32[2048,1,128]{0,2,1:T(8,128)}, ...), condition=%wide.region_7.9_spmd.clone, body=%wide.region_2.8_spmd.clone.sunk | while | flops 814710016 | bytes 48644448 | solution.py:77
  575.2 1.9 fusion.68
  577.8 1.4 fusion.69
  586.8 1.9 fusion.68
  598.4 1.9 fusion.68
  610.1 1.9 fusion.68
  612.7 1.4 fusion.69
  621.7 1.9 fusion.68
  633.3 1.9 fusion.68
  635.9 1.4 fusion.69
  644.9 1.9 fusion.68
  656.5 1.9 fusion.68
  665.3 1.6 copy.40
  668.3 1.4 maximum_select_fusion
  669.8 2.5 broadcast_in_dim.68
  672.2 6.4 scatter_fusion
  678.6 7.4 all-to-all-start
  686.0 186.7 %psum.7 = f32[]{:T(128)} all-reduce(f32[]{:T(128)} %get-tuple-element.72), channel_id=1, replica_groups=mesh['ctx'=64,'tp'=8] {'ctx','tp'}, use_global_device_ids=true, to_apply=%region_10.12 | all-reduce | flops 1 | bytes 8 | tf_op jit(solution)/shard_map/psum | solution.py:96
  874.6 2.4 reduce_sum.36
  (205 shorter events, 77.7 us)
Async XLA Ops:
  7.2 6.5 copy-start
  7.2 9.2 %copy-start.8 = (bf16[256,1024]{1,0:T(8,128)(2,1)S(1)}, bf16[256,1024]{1,0:T(8,128)(2,1)}, u32[]{:S(2)}) copy-start(bf16[256,1024]{1,0:T(8,128)(2,1)} %param.12) | copy-start | bytes 1572868
  7.2 263.5 %all-gather.5.cloned.1.call-start = ((), (), s32[]{:S(2)}) async-start(), calls=%async_computation.2 | async-start | bytes 1064960 | tf_op jit(solution)/shard_map/all_gather | solution.py:21
  7.9 562.4 %all-gather.3.cloned.1.call-start = ((), (), s32[]{:S(2)}) async-start(), calls=%async_computation.1 | async-start | bytes 1064960 | tf_op jit(solution)/shard_map/all_gather | solution.py:20
  579.3 2.5 copy-start.4
  580.7 2.4 copy-start.2
  580.7 3.4 copy-start.7
  590.9 2.5 copy-start.4
  592.3 3.4 copy-start.7
  602.5 2.5 copy-start.4
  603.9 2.4 copy-start.2
  603.9 3.4 copy-start.7
  614.1 2.5 copy-start.4
  615.5 3.4 copy-start.7
  625.7 2.5 copy-start.4
  627.1 3.4 copy-start.7
  637.3 2.5 copy-start.4
  638.7 3.4 copy-start.7
  649.0 2.5 copy-start.4
  650.4 3.4 copy-start.7
  660.6 2.5 copy-start.4
  662.0 3.4 copy-start.7
  678.6 194.1 %copy-start.9 = (bf16[8,256,1,128]{3,1,2,0:T(8,128)(2,1)S(1)}, bf16[8,256,1,128]{3,1,2,0:T(8,128)(2,1)}, u32[]{:S(2)}) copy-start(bf16[8,256,1,128]{3,1,2,0:T(8,128)(2,1)} %get-tuple-element.69) | copy-start | bytes 1572868
  678.6 196.0 %all-to-all-start = ((f32[64,64,256]{2,1,0:T(8,128)}), f32[64,64,256]{2,1,0:T(8,128)}, u32[]{:S(2)}, u32[]{:S(2)}) async-start(f32[64,64,256]{2,1,0:T(8,128)} %scatter_fusion), calls=%async_computation | async-start | bytes 8388608 | tf_op jit(solution)/shard_map/all_to_all | solution.py:92
  (31 other events, 46.7 us)
Sparse Core Ops, SparseCore 0:
  10.1 260.5 all-gather.4
  272.8 297.4 all-gather.2
where the time goes:
time: 887 us; the launch traced here: 886 us
  waiting for transfers between devices  552 us (62%)
  blocking collectives  187 us (21%)
  matrix products  61.8 us (7%)
  local copies, waits for them, and re-layouts  30.3 us (3%)
  other arithmetic  24.2 us (3%)
  between operations  16.7 us (2%)
    all_gather x1, waiting for transfers between devices, per_device(): lax.all_gather(image_keys, 'ctx', axis=0, tiled=True)  298 us
    all_gather x1, waiting for transfers between devices, per_device(): lax.all_gather(image_values, 'ctx', axis=0, tiled=True)  253 us
    psum x1, blocking collectives, per_device(): gate_total = lax.psum(gate_acc, ('ctx', 'tp'))  187 us
  transfers between devices with their start and end apart: 3, of which 2 were waited for; matrix products, arithmetic and copies ran while one was open for 1% of the time, Pallas kernels for 0%

commit v1 on v0

--- a/solution.py
+++ b/solution.py
@@ -93,7 +93,8 @@
     summed = jnp.sum(received, axis=0, keepdims=True)
     key_grad = summed[:, :, : local_kv * HD].astype(jnp.bfloat16)
     value_grad = summed[:, :, local_kv * HD :].astype(jnp.bfloat16)
-    gate_total = lax.psum(gate_acc, ("ctx", "tp"))
+    b_now = lax.all_gather(gate_acc, ("ctx", "tp"))
+    gate_total = jnp.sum(b_now, axis=0)
     term_count = tok_dev * lax.axis_size("ctx") * local_heads * lax.axis_size("tp") * HD
     gate_grad = ((1.0 - gate_value * gate_value) * gate_total / math.sqrt(term_count)).reshape(1)
     return (query_grad, key_grad, value_grad, gate_grad)

time: 887 us -> 888 us (level)
    psum x1 -> x0, blocking collectives: 187 us -> none  [per_device(): gate_total = lax.psum(gate_acc, ('ctx', 'tp'))]
    unnamed x0 -> x1, blocking collectives: none -> 187 us
where the time goes in v1:
time: 888 us; the launch traced here: 886 us
  waiting for transfers between devices  552 us (62%)
  blocking collectives  187 us (21%)
  matrix products  61.8 us (7%)
  local copies, waits for them, and re-layouts  30.4 us (3%)
  other arithmetic  24.8 us (3%)
  between operations  16.7 us (2%)
    all_gather x1, waiting for transfers between devices, per_device(): lax.all_gather(image_keys, 'ctx', axis=0, tiled=True)  298 us
    all_gather x1, waiting for transfers between devices, per_device(): lax.all_gather(image_values, 'ctx', axis=0, tiled=True)  253 us
    unnamed x1, blocking collectives  187 us
  transfers between devices with their start and end apart: 3, of which 2 were waited for; matrix products, arithmetic and copies ran while one was open for 1% of the time, Pallas kernels for 0%

profile of v1, /device:TPU:1, one launch (start us, length us, event | category | flops | bytes accessed | tf_op | source)
XLA Modules:
  0.0 886.3 jit_solution(6285216931357811261)
XLA Ops:
  10.9 2.0 top_k.11
  17.4 253.3 %all-gather.5.cloned.1.call-done = bf16[64,64,128]{2,1,0:T(8,128)(2,1)} async-done(((bf16[1,64,128]{2,1,0:T(8,128)(2,1)}), bf16[64,64,128]{2,1,0:T(8,128)(2,1)}) %all-gather.5.cloned.1.call-update) | async-done | bytes 1048592 | tf_op jit(solution)/shard_map/all_gather | solution.py:21
  270.7 1.9 gather_fusion.4
  272.6 297.7 %all-gather.3.cloned.1.call-done = bf16[64,64,128]{2,1,0:T(8,128)(2,1)} async-done(((bf16[1,64,128]{2,1,0:T(8,128)(2,1)}), bf16[64,64,128]{2,1,0:T(8,128)(2,1)}) %all-gather.3.cloned.1.call-update) | async-done | bytes 1048592 | tf_op jit(solution)/shard_map/all_gather | solution.py:20
  570.4 1.9 gather_fusion.3
  572.4 92.9 %while.17 = (s32[]{:T(128)}, f32[2048,1,128]{0,2,1:T(8,128)}, f32[2048,1,128]{0,2,1:T(8,128)}, f32[]{:T(128)}, bf16[8,256,1,128]{3,1,2,0:T(8,128)(2,1)}, /*index...) while((s32[]{:T(128)}, f32[2048,1,128]{0,2,1:T(8,128)}, ...), condition=%wide.region_7.9_spmd.clone, body=%wide.region_2.8_spmd.clone.sunk | while | flops 814710016 | bytes 48644448 | solution.py:77
  575.2 1.9 fusion.68
  577.8 1.4 fusion.69
  586.8 1.9 fusion.68
  598.4 1.9 fusion.68
  610.1 1.9 fusion.68
  612.7 1.4 fusion.69
  621.7 1.9 fusion.68
  633.3 1.9 fusion.68
  635.9 1.4 fusion.69
  644.9 1.9 fusion.68
  656.5 1.9 fusion.68
  665.3 1.6 copy.40
  668.3 1.4 maximum_select_fusion
  669.8 2.5 broadcast_in_dim.68
  672.2 6.4 scatter_fusion
  678.6 7.4 all-to-all-start
  686.1 186.6 %all-reduce = f32[512]{0:T(512)S(1)} all-reduce(f32[512]{0:T(512)S(1)} %dynamic-update-slice), channel_id=1, replica_groups=mesh['ctx'=64,'tp'=8] {'ctx','tp'}, use_global_device_ids=true, to_apply=%add | all-reduce | flops 512 | bytes 4096
  875.3 2.4 reduce_sum.45
  (208 shorter events, 78.4 us)
Async XLA Ops:
  7.2 6.5 copy-start
  7.2 9.2 %copy-start.8 = (bf16[256,1024]{1,0:T(8,128)(2,1)S(1)}, bf16[256,1024]{1,0:T(8,128)(2,1)}, u32[]{:S(2)}) copy-start(bf16[256,1024]{1,0:T(8,128)(2,1)} %param.12) | copy-start | bytes 1572868
  7.2 263.5 %all-gather.5.cloned.1.call-start = ((), (), s32[]{:S(2)}) async-start(), calls=%async_computation.2 | async-start | bytes 1064960 | tf_op jit(solution)/shard_map/all_gather | solution.py:21
  7.9 562.4 %all-gather.3.cloned.1.call-start = ((), (), s32[]{:S(2)}) async-start(), calls=%async_computation.1 | async-start | bytes 1064960 | tf_op jit(solution)/shard_map/all_gather | solution.py:20
  579.3 2.5 copy-start.4
  580.7 2.4 copy-start.2
  580.7 3.4 copy-start.7
  590.9 2.5 copy-start.4
  592.3 3.4 copy-start.7
  602.5 2.5 copy-start.4
  603.9 2.4 copy-start.2
  603.9 3.4 copy-start.7
  614.1 2.5 copy-start.4
  615.5 3.4 copy-start.7
  625.7 2.5 copy-start.4
  627.1 3.4 copy-start.7
  637.3 2.5 copy-start.4
  638.7 3.4 copy-start.7
  649.0 2.5 copy-start.4
  650.4 3.4 copy-start.7
  660.6 2.5 copy-start.4
  662.0 3.4 copy-start.7
  678.6 194.7 %copy-start.9 = (bf16[8,256,1,128]{3,1,2,0:T(8,128)(2,1)S(1)}, bf16[8,256,1,128]{3,1,2,0:T(8,128)(2,1)}, u32[]{:S(2)}) copy-start(bf16[8,256,1,128]{3,1,2,0:T(8,128)(2,1)} %get-tuple-element.69) | copy-start | bytes 1572868
  678.6 196.6 %all-to-all-start = ((f32[64,64,256]{2,1,0:T(8,128)}), f32[64,64,256]{2,1,0:T(8,128)}, u32[]{:S(2)}, u32[]{:S(2)}) async-start(f32[64,64,256]{2,1,0:T(8,128)} %scatter_fusion), calls=%async_computation | async-start | bytes 8388608 | tf_op jit(solution)/shard_map/all_to_all | solution.py:92
  (31 other events, 46.7 us)
Sparse Core Ops, SparseCore 0:
  10.1 260.5 all-gather.4
  272.8 297.4 all-gather.2

commit v2 on v0

--- a/solution.py
+++ b/solution.py
@@ -17,7 +17,15 @@
     inv_root = 1.0 / math.sqrt(HD)
     read_most = lax.axis_size("ctx") // 2
     gathered_keys, gathered_values = (
-        lax.all_gather(image_keys, "ctx", axis=0, tiled=True),
+        jnp.concatenate(
+            lax.all_to_all(
+                jnp.stack(lax.axis_size("ctx") * [image_keys], axis=0),
+                axis_name="ctx",
+                split_axis=0,
+                concat_axis=0,
+            ),
+            axis=0,
+        ),
         lax.all_gather(image_values, "ctx", axis=0, tiled=True),
     )
     n_images = gathered_keys.shape[0]

time: 887 us -> 601 us (0.68)
  waiting for transfers between devices: 552 us -> 251 us
  starting transfers between devices: 7.46 us -> 23 us
    all_gather x1 -> x0, waiting for transfers between devices: 298 us -> none  [per_device(): lax.all_gather(image_keys, 'ctx', axis=0, tiled=True)]
    all_gather x1, waiting for transfers between devices: 253 us -> 234 us  [per_device(): lax.all_gather(image_values, 'ctx', axis=0, tiled=True)]
    all_to_all x0 -> x1, waiting for transfers between devices: none -> 16.4 us  [per_device(): lax.all_to_all(jnp.stack(lax.axis_size('ctx') * [image_keys], axis=0), ax...]
    all_to_all x0 -> x1, starting transfers between devices: none -> 15.5 us  [per_device(): lax.all_to_all(jnp.stack(lax.axis_size('ctx') * [image_keys], axis=0), ax...]
where the time goes in v2:
time: 601 us; the launch traced here: 600 us
  waiting for transfers between devices  251 us (42%)
  blocking collectives  188 us (31%)
  matrix products  61.8 us (10%)
  local copies, waits for them, and re-layouts  29.4 us (5%)
  other arithmetic  23.5 us (4%)
  starting transfers between devices  23 us (4%)
  between operations  16.7 us (3%)
  loops' own time  6.11 us (1%)
    all_gather x1, waiting for transfers between devices, per_device(): lax.all_gather(image_values, 'ctx', axis=0, tiled=True)  234 us
    psum x1, blocking collectives, per_device(): gate_total = lax.psum(gate_acc, ('ctx', 'tp'))  188 us
    all_to_all x1, waiting for transfers between devices, per_device(): lax.all_to_all(jnp.stack(lax.axis_size('ctx') * [image_keys], axis=0), ax...  16.4 us
    dot_general x8, matrix products, head_step(): jnp.einsum('kts,skd->tkd', prob_half, value_rows, preferred_element_type=...  15.5 us
    all_to_all x1, starting transfers between devices, per_device(): lax.all_to_all(jnp.stack(lax.axis_size('ctx') * [image_keys], axis=0), ax...  15.5 us
  transfers between devices with their start and end apart: 3, of which 2 were waited for; matrix products, arithmetic and copies ran while one was open for 1% of the time, Pallas kernels for 0%

profile of v2, /device:TPU:1, one launch (start us, length us, event | category | flops | bytes accessed | tf_op | source)
XLA Modules:
  0.0 599.6 jit_solution(14130284305143471469)
XLA Ops:
  7.2 2.0 stack.2
  9.2 15.5 %all-to-all-start = ((bf16[64,1,64,128]{3,2,1,0:T(8,128)(2,1)}), bf16[64,1,64,128]{3,2,1,0:T(8,128)(2,1)S(1)}, u32[]{:S(2)}, u32[]{:S(2)}) async-start(bf16[64,1,64,128]{3,2,1,0:T(8,128)(2,1)} %stack.2), calls=%async_computation | async-start | bytes 2097152 | tf_op jit(solution)/shard_map/all_to_all | solution.py:21
  26.3 2.0 top_k.11
  31.8 16.4 %all-to-all-done = bf16[64,1,64,128]{3,2,1,0:T(8,128)(2,1)S(1)} async-done(((bf16[64,1,64,128]{3,2,1,0:T(8,128)(2,1)}), bf16[64,1,64,128]{3,2,1,0:T(8,128)(2,1)S(1)}, u32[]{:S(2)}, u32[]{:S(2)}) %all-to-all-start) | async-done | bytes 1048608 | tf_op jit(solution)/shard_map/all_to_all | solution.py:21
  48.9 233.9 %all-gather.2.cloned.1.call-done = bf16[64,64,128]{2,1,0:T(8,128)(2,1)} async-done(((bf16[1,64,128]{2,1,0:T(8,128)(2,1)}), bf16[64,64,128]{2,1,0:T(8,128)(2,1)}) %all-gather.2.cloned.1.call-update) | async-done | bytes 1048592 | tf_op jit(solution)/shard_map/all_gather | solution.py:29
  282.8 1.9 gather_fusion.4
  284.9 92.9 %while.17 = (s32[]{:T(128)}, f32[2048,1,128]{0,2,1:T(8,128)}, f32[2048,1,128]{0,2,1:T(8,128)}, f32[]{:T(128)}, bf16[8,256,1,128]{3,1,2,0:T(8,128)(2,1)}, /*index...) while((s32[]{:T(128)}, f32[2048,1,128]{0,2,1:T(8,128)}, ...), condition=%wide.region_7.9_spmd.clone, body=%wide.region_2.8_spmd.clone.sunk | while | flops 814710016 | bytes 48644448 | solution.py:85
  287.7 1.9 fusion.68
  299.3 1.9 fusion.68
  310.9 1.9 fusion.68
  322.5 1.9 fusion.68
  325.1 1.4 fusion.69
  334.1 1.9 fusion.68
  345.8 1.9 fusion.68
  348.4 1.4 fusion.69
  357.4 1.9 fusion.68
  369.0 1.9 fusion.68
  377.8 1.6 copy.40
  380.8 1.4 maximum_select_fusion
  382.2 2.5 broadcast_in_dim.68
  384.7 6.4 %scatter_fusion = f32[64,64,256]{2,1,0:T(8,128)} fusion(f32[64,64,256]{2,1,0:T(8,128)} %broadcast_in_dim.68, s32[32]{0:T(128)S(1)} %fusion.36, f32[32,64,256]{2,1,0:T(8,128)S(1)} %maximum_select_fusion), kind=kCustom, calls=%fused_computation.5 | custom fusion | flops 524288 | bytes 6291584 | tf_op jit(solution)/shard_map/scatter-add | solution.py:98
  391.1 7.5 %all-to-all-start.1 = ((f32[64,64,256]{2,1,0:T(8,128)}), f32[64,64,256]{2,1,0:T(8,128)}, u32[]{:S(2)}, u32[]{:S(2)}) async-start(f32[64,64,256]{2,1,0:T(8,128)} %scatter_fusion), calls=%async_computation.1 | async-start | bytes 8388608 | tf_op jit(solution)/shard_map/all_to_all | solution.py:100
  398.6 188.1 %psum.7 = f32[]{:T(128)} all-reduce(f32[]{:T(128)} %get-tuple-element.72), channel_id=1, replica_groups=mesh['ctx'=64,'tp'=8] {'ctx','tp'}, use_global_device_ids=true, to_apply=%region_10.12 | all-reduce | flops 1 | bytes 8 | tf_op jit(solution)/shard_map/psum | solution.py:104
  588.6 2.4 reduce_sum.36
  (209 shorter events, 76.7 us)
Async XLA Ops:
  7.2 21.9 %copy-start = (s32[64]{0:T(128)S(1)}, s32[64]{0:T(128)}, u32[]{:S(2)}) copy-start(s32[64]{0:T(128)} %param.17) | copy-start | bytes 772
  7.2 19.0 %copy-start.11 = (s32[2,64]{1,0:T(2,128)S(1)}, s32[2,64]{1,0:T(2,128)}, u32[]{:S(2)}) copy-start(s32[2,64]{1,0:T(2,128)} %param.16) | copy-start | bytes 1540
  7.2 23.4 %copy-start.8 = (bf16[256,1024]{1,0:T(8,128)(2,1)S(1)}, bf16[256,1024]{1,0:T(8,128)(2,1)}, u32[]{:S(2)}) copy-start(bf16[256,1024]{1,0:T(8,128)(2,1)} %param.11) | copy-start | bytes 1572868
  9.2 21.6 %copy-start.9 = (bf16[256,1024]{1,0:T(8,128)(2,1)S(1)}, bf16[256,1024]{1,0:T(8,128)(2,1)}, u32[]{:S(2)}) copy-start(bf16[256,1024]{1,0:T(8,128)(2,1)} %param.12) | copy-start | bytes 1572868
  9.2 39.0 %all-to-all-start = ((bf16[64,1,64,128]{3,2,1,0:T(8,128)(2,1)}), bf16[64,1,64,128]{3,2,1,0:T(8,128)(2,1)S(1)}, u32[]{:S(2)}, u32[]{:S(2)}) async-start(bf16[64,1,64,128]{3,2,1,0:T(8,128)(2,1)} %stack.2), calls=%async_computation | async-start | bytes 2097152 | tf_op jit(solution)/shard_map/all_to_all | solution.py:21
  24.7 258.1 %all-gather.2.cloned.1.call-start = ((), (), s32[]{:S(2)}) async-start(), calls=%async_computation.2 | async-start | bytes 1064960 | tf_op jit(solution)/shard_map/all_gather | solution.py:29
  291.8 2.5 copy-start.4
  293.2 3.4 copy-start.7
  303.4 2.5 copy-start.4
  304.8 3.4 copy-start.7
  315.0 2.5 copy-start.4
  316.4 3.4 copy-start.7
  326.6 2.5 copy-start.4
  328.0 3.4 copy-start.7
  338.2 2.5 copy-start.4
  339.6 3.4 copy-start.7
  349.8 2.5 copy-start.4
  351.2 3.4 copy-start.7
  361.4 2.5 copy-start.4
  362.8 3.4 copy-start.7
  373.0 2.5 copy-start.4
  374.4 3.4 copy-start.7
  391.1 195.6 %copy-start.10 = (bf16[8,256,1,128]{3,1,2,0:T(8,128)(2,1)S(1)}, bf16[8,256,1,128]{3,1,2,0:T(8,128)(2,1)}, u32[]{:S(2)}) copy-start(bf16[8,256,1,128]{3,1,2,0:T(8,128)(2,1)} %get-tuple-element.69) | copy-start | bytes 1572868
  391.1 197.5 %all-to-all-start.1 = ((f32[64,64,256]{2,1,0:T(8,128)}), f32[64,64,256]{2,1,0:T(8,128)}, u32[]{:S(2)}, u32[]{:S(2)}) async-start(f32[64,64,256]{2,1,0:T(8,128)} %scatter_fusion), calls=%async_computation.1 | async-start | bytes 8388608 | tf_op jit(solution)/shard_map/all_to_all | solution.py:100
  (33 other events, 51.5 us)
Sparse Core Ops, SparseCore 0:
  27.6 255.1 all-gather.1
